TPU v7x, 32 devices: a whole 2x2x4 slice. The times are simulated.
32 devices in a mesh: groups: 2 (over y), tensor: 8 (over z, x), dp: 2 (over core).
Axes of the slice: x: 2, y: 2, z: 4, core: 2. Of those that a mesh axis runs over, the one named last changes fastest.
Arguments:
- gate_pre: bfloat16 [2048, 28672], P(('groups', 'dp'), 'tensor'), parts along dimension 0, may hold values from -6 to 6
- up_pre: bfloat16 [2048, 28672], P(('groups', 'dp'), 'tensor'), parts along dimension 0, may hold values from -16 to 16
- down_weight: bfloat16 [28672, 4096], P('tensor'), may hold values from -0.375 to 0.375
- out_grad: bfloat16 [2048, 4096], P(('groups', 'dp'), 'tensor'), parts along dimension 0, may hold values from -2.5 to 2.5
Outputs:
- grad_gate: bfloat16 [2048, 28672], P(('groups', 'dp'), 'tensor'), parts along dimension 0
- grad_up: bfloat16 [2048, 28672], P(('groups', 'dp'), 'tensor'), parts along dimension 0
- grad_down: bfloat16 [57344, 4096], P(('groups', 'tensor'), 'dp'), parts along dimension 0
There are 2 independent parts, one for each index of `groups`. A program takes and returns all parts, laid end to end along the dimension named above; an argument that names none is the same for every part. Nothing has to cross between parts.
All inputs are finite; a program needn't handle non-finite values.
Results may differ from a plain program's by a relative error of at most 0.0061.
Values may be sent and summed in bfloat16 or wider, within the bound.
A program may use at most 320 MiB of HBM per device.

v0:
```python
import math

import jax
import jax.numpy as jnp
import numpy as np
from jax import lax
from jax.sharding import PartitionSpec as P

HAD_LARGE = 1024
GROUP = 128


def paley_table():
    residues = set((number * number % 13 for number in range(1, 13)))
    core_matrix = np.zeros((14, 14))
    core_matrix[0, 1:] = 1.0
    core_matrix[1:, 0] = 1.0
    for row_index in range(13):
        for col_index in range(13):
            offset = (col_index - row_index) % 13
            if offset != 0:
                core_matrix[row_index + 1, col_index + 1] = 1.0 if offset in residues else -1.0
    upper_block = np.array([[1.0, 1.0], [1.0, -1.0]])
    diagonal_block = np.array([[1.0, -1.0], [-1.0, -1.0]])
    return np.kron(core_matrix, upper_block) + np.kron(np.eye(14), diagonal_block)


def sylvester(matrix_order):
    positions = jnp.arange(matrix_order, dtype=jnp.int32)
    common_bits = jnp.bitwise_and(positions[:, None], positions[None, :])
    parity = jnp.zeros((matrix_order, matrix_order), jnp.int32)
    for bit_shift in range(matrix_order.bit_length() - 1):
        parity = parity + jnp.bitwise_and(jnp.right_shift(common_bits, bit_shift), 1)
    return (1 - 2 * (parity % 2)).astype(jnp.float32)


def rotate(rows_in, small_table, large_table):
    row_count, width = rows_in.shape
    large_order = large_table.shape[0]
    small_order = small_table.shape[0]
    first_section = jnp.dot(
        rows_in.reshape(row_count * small_order, large_order),
        large_table,
        preferred_element_type=jnp.float32,
    )
    first_section = first_section.reshape(row_count, small_order, large_order)
    rotated = jnp.einsum("ac,tad->tcd", small_table, first_section, precision=lax.Precision.HIGHEST)
    return rotated.reshape(row_count, width) * (1.0 / math.sqrt(width))


def quantize(rotated):
    grouped = rotated.reshape(rotated.shape[0], -1, GROUP)
    largest = jnp.max(jnp.abs(grouped), axis=-1, keepdims=True)
    spacing = largest * (0.9 / 7.0) + 1e-06
    scaled = grouped / spacing
    staircase = jnp.minimum(scaled - jnp.sin(2.0 * math.pi * scaled) / (2.0 * math.pi), 7.0)
    return (staircase * spacing).reshape(rotated.shape).astype(jnp.bfloat16)


def per_device(gate_pre, up_pre, down_weight, out_grad):
    small_table = jnp.asarray(paley_table(), jnp.float32)
    large_table = sylvester(HAD_LARGE).astype(jnp.bfloat16)
    gate_wide = gate_pre.astype(jnp.float32)
    up_wide = up_pre.astype(jnp.float32)
    sigmoid_gate = jax.nn.sigmoid(gate_wide)
    activated = gate_wide * sigmoid_gate
    hidden = (activated * up_wide).astype(jnp.bfloat16)
    full_grad = lax.all_gather(out_grad, "tensor", axis=1, tiled=True)
    rot_grad = lax.dot_general(
        full_grad, down_weight, (((1,), (1,)), ((), ())), preferred_element_type=jnp.float32
    ).astype(jnp.bfloat16)
    token_hidden = lax.all_to_all(hidden, "tensor", split_axis=0, concat_axis=1, tiled=True)
    quant_rows = quantize(rotate(token_hidden, small_table, large_table))
    quantized = lax.all_to_all(quant_rows, "tensor", split_axis=1, concat_axis=0, tiled=True)
    token_grad = lax.all_to_all(rot_grad, "tensor", split_axis=0, concat_axis=1, tiled=True)
    back_rows = rotate(token_grad, small_table.T, large_table.T).astype(jnp.bfloat16)
    hidden_grad = lax.all_to_all(back_rows, "tensor", split_axis=1, concat_axis=0, tiled=True)
    partial_grad = lax.dot_general(
        quantized, full_grad, (((0,), (0,)), ((), ())), preferred_element_type=jnp.float32
    )
    grad_down = lax.psum_scatter(partial_grad, "dp", scatter_dimension=1, tiled=True).astype(
        jnp.bfloat16
    )
    hid_wide = hidden_grad.astype(jnp.float32)
    grad_up = (hid_wide * activated).astype(jnp.bfloat16)
    grad_gate = (
        hid_wide * up_wide * sigmoid_gate * (1.0 + gate_wide * (1.0 - sigmoid_gate))
    ).astype(jnp.bfloat16)
    return (grad_gate, grad_up, grad_down)


def solution(mesh):
    return jax.shard_map(
        per_device,
        mesh=mesh,
        in_specs=(
            P(("groups", "dp"), "tensor"),
            P(("groups", "dp"), "tensor"),
            P("tensor", None),
            P(("groups", "dp"), "tensor"),
        ),
        out_specs=(
            P(("groups", "dp"), "tensor"),
            P(("groups", "dp"), "tensor"),
            P(("groups", "tensor"), "dp"),
        ),
        check_vma=False,
    )
```

profile of v0, /device:TPU:16, one launch (start us, length us, event | category | flops | bytes accessed | tf_op | source)
XLA Modules:
  0.0 734.2 jit_solution(4318890559414260404)
XLA Ops:
  7.9 77.3 %all-gather.2.cloned.1.call-done = bf16[512,4096]{1,0:T(8,128)(2,1)} async-done(((bf16[512,512]{1,0:T(8,128)(2,1)}), bf16[512,4096]{1,0:T(8,128)(2,1)}) %all-gather.2.cloned.1.call-update) | async-done | bytes 4194320 | tf_op jit(solution)/shard_map/all_gather | solution.py:68
  85.3 23.0 %convolution_convert_fusion = bf16[512,3584]{1,0:T(8,128)(2,1)} fusion(bf16[512,4096]{1,0:T(8,128)(2,1)} %all-gather.2.cloned.1.call-done, bf16[3584,4096]{1,0:T(8,128)(2,1)} %param.7), kind=kOutput, calls=%fused_computation.26 | convolution fusion | flops 15034220544 | bytes 37224448 | tf_op jit(solution)/shard_map/dot_general | solution.py:69
  108.3 84.9 %all_to_all.58 = bf16[8,64,3584]{2,1,0:T(8,128)(2,1)S(1)} all-to-all(bf16[8,64,3584]{2,1,0:T(8,128)(2,1)} %bitcast.36), channel_id=1, replica_groups=mesh['groups'=2,'tensor'=8,'dp'=2] {'tensor'}, dimensions={0} | all-to-all | bytes 7340032 | tf_op jit(solution)/shard_map/all_to_all | solution.py:75
  193.2 3.8 copy.23
  197.0 8.1 %dot_general.23 = bf16[64,28,1024]{2,1,0:T(8,128)(2,1)} reshape(bf16[64,8,3584]{2,1,0:T(8,128)(2,1)} %copy.23) | data formatting | bytes 7340032 | tf_op jit(solution)/shard_map/dot_general | solution.py:41
  205.1 13.2 %fusion.21 = f32[64,28,1024]{2,0,1:T(8,128)S(1)} fusion(bf16[64,28,1024]{2,1,0:T(8,128)(2,1)} %dot_general.23), kind=kOutput, calls=%fused_computation.35 | convolution fusion | flops 3805282304 | bytes 11010048 | tf_op jit(solution)/shard_map/dot_general | solution.py:41
  218.3 15.1 %fusion.18 = bf16[64,28,1024]{2,1,0:T(8,128)(2,1)} fusion(f32[28,28,1]{1,0,2:T(8,128)S(1)} %copy-done.2, f32[64,28,1024]{2,0,1:T(8,128)S(1)} %fusion.21), kind=kOutput, calls=%fused_computation.32 | convolution fusion | flops 620232704 | bytes 11013184 | tf_op jit(solution)/shard_map/ac,tad->tcd/dot_general | solution.py:47
  233.4 7.9 %convert_element_type.59 = bf16[64,8,3584]{2,1,0:T(8,128)(2,1)} reshape(bf16[64,28,1024]{2,1,0:T(8,128)(2,1)} %fusion.18) | data formatting | bytes 7340032 | tf_op jit(solution)/shard_map/convert_element_type | solution.py:76
  244.5 85.1 %all_to_all.59 = bf16[64,8,3584]{2,0,1:T(8,128)(2,1)S(1)} all-to-all(bf16[64,8,3584]{2,0,1:T(8,128)(2,1)S(1)} %copy.26), channel_id=1, replica_groups=mesh['groups'=2,'tensor'=8,'dp'=2] {'tensor'}, dimensions={1} | all-to-all | bytes 7340032 | tf_op jit(solution)/shard_map/all_to_all | solution.py:77
  329.6 6.4 fusion.7
  336.0 85.0 %all_to_all.60 = bf16[8,64,3584]{2,1,0:T(8,128)(2,1)S(1)} all-to-all(bf16[8,64,3584]{2,1,0:T(8,128)(2,1)S(1)} %bitcast.34), channel_id=1, replica_groups=mesh['groups'=2,'tensor'=8,'dp'=2] {'tensor'}, dimensions={0} | all-to-all | bytes 7340032 | tf_op jit(solution)/shard_map/all_to_all | solution.py:72
  424.8 7.9 %dot_general.26 = bf16[64,28,1024]{2,1,0:T(8,128)(2,1)} reshape(bf16[64,8,3584]{2,1,0:T(8,128)(2,1)} %copy.27) | data formatting | bytes 7340032 | tf_op jit(solution)/shard_map/dot_general | solution.py:41
  432.7 13.2 %fusion.19 = f32[64,28,1024]{2,0,1:T(8,128)S(1)} fusion(bf16[64,28,1024]{2,1,0:T(8,128)(2,1)} %dot_general.26), kind=kOutput, calls=%fused_computation.33 | convolution fusion | flops 3805282304 | bytes 11010048 | tf_op jit(solution)/shard_map/dot_general | solution.py:41
  445.9 17.9 %multiply_bitcast_fusion = (f32[64,28,1024]{2,1,0:T(8,128)}, f32[64,28,1024]{2,1,0:T(8,128)}) fusion(f32[28,28,1]{1,0,2:T(8,128)S(1)} %copy-done.2, f32[64,28,1024]{2,0,1:T(8,128)S(1)} %fusion.19), kind=kOutput, calls=%fused_computation.11 | convolution fusion | flops 620232704 | bytes 22023232 | tf_op jit(solution)/shard_map/ac,tad->tcd/dot_general | solution.py:47
  463.8 10.1 %mul.81 = f32[64,8,3584]{2,1,0:T(8,128)} reshape(f32[64,28,1024]{2,1,0:T(8,128)} %get-tuple-element.3) | data formatting | bytes 14680064 | tf_op jit(solution)/shard_map/mul | solution.py:48
  473.8 9.1 %abs.11 = f32[64,224,128]{2,1,0:T(8,128)} reshape(f32[64,28,1024]{2,1,0:T(8,128)} %get-tuple-element.4) | data formatting | bytes 14680064 | tf_op jit(solution)/shard_map/abs | solution.py:53
  482.9 5.3 reduce_max.9
  488.3 4.2 div.19
  492.4 8.3 %div.20 = f32[64,8,3584]{2,1,0:T(8,128)} reshape(f32[64,224,128]{2,1,0:T(8,128)} %div.19) | data formatting | bytes 14680064 | tf_op jit(solution)/shard_map/div | solution.py:55
  500.7 27.0 %multiply_convert_fusion.1 = bf16[64,8,3584]{2,1,0:T(8,128)(2,1)S(1)} fusion(f32[64,8,3584]{2,1,0:T(8,128)} %div.20, f32[64,8,3584]{2,1,0:T(8,128)} %mul.81), kind=kLoop, calls=%fused_computation.22 | loop fusion | flops 12845056 | bytes 18350080 | tf_op jit(solution)/shard_map/convert_element_type | solution.py:57
  528.8 85.1 %all_to_all.61 = bf16[64,8,3584]{2,0,1:T(8,128)(2,1)S(1)} all-to-all(bf16[64,8,3584]{2,0,1:T(8,128)(2,1)S(1)} %copy.31), channel_id=1, replica_groups=mesh['groups'=2,'tensor'=8,'dp'=2] {'tensor'}, dimensions={1} | all-to-all | bytes 7340032 | tf_op jit(solution)/shard_map/all_to_all | solution.py:74
  613.9 22.8 %fusion.56 = f32[3584,4096]{1,0:T(8,128)} fusion(bf16[512,3584]{1,0:T(8,128)(2,1)S(1)} %bitcast.35, bf16[512,4096]{1,0:T(8,128)(2,1)S(1)} %copy-done.3), kind=kOutput, calls=%fused_computation.65 | convolution fusion | flops 15032385536 | bytes 66584576 | tf_op jit(solution)/shard_map/dot_general | solution.py:78
  636.7 73.7 %reduce-scatter.2.cloned.1.call-done = f32[3584,2048]{1,0:T(8,128)} async-done(((f32[3584,4096]{1,0:T(8,128)}), f32[3584,2048]{1,0:T(8,128)}) %reduce-scatter.2.cloned.1.call-update) | async-done | bytes 29360144 | tf_op jit(solution)/shard_map/reduce_scatter | solution.py:81
  710.4 16.5 %convert_element_type.69 = bf16[3584,2048]{1,0:T(8,128)(2,1)} convert(f32[3584,2048]{1,0:T(8,128)} %reduce-scatter.2.cloned.1.call-done) | non-fusion elementwise | flops 7340032 | bytes 44040192 | tf_op jit(solution)/shard_map/convert_element_type | solution.py:81
  (16 shorter events, 8.8 us)
Async XLA Ops:
  7.2 78.1 %all-gather.2.cloned.1.call-start = ((), (), s32[]{:S(2)}) async-start(), calls=%async_computation.5 | async-start | bytes 4718592 | tf_op jit(solution)/shard_map/all_gather | solution.py:68
  7.9 702.5 %reduce-scatter.2.cloned.1.call-start = ((), (), s32[]{:S(2)}) async-start(), calls=%async_computation.6 | async-start | bytes 88080384 | tf_op jit(solution)/shard_map/reduce_scatter | solution.py:81
  205.1 13.2 %copy-start.2 = (f32[28,28,1]{1,0,2:T(8,128)S(1)}, f32[28,28,1]{1,0,2:T(8,128)}, u32[]{:S(2)}) copy-start(f32[28,28,1]{1,0,2:T(8,128)} %constant.51) | copy-start | bytes 9412
  244.5 85.1 %copy-start = (bf16[512,3584]{1,0:T(8,128)(2,1)S(1)}, bf16[512,3584]{1,0:T(8,128)(2,1)}, u32[]{:S(2)}) copy-start(bf16[512,3584]{1,0:T(8,128)(2,1)} %param.6) | copy-start | bytes 11010052
  244.5 85.1 %copy-start.1 = (bf16[512,3584]{1,0:T(8,128)(2,1)S(1)}, bf16[512,3584]{1,0:T(8,128)(2,1)}, u32[]{:S(2)}) copy-start(bf16[512,3584]{1,0:T(8,128)(2,1)} %param.5) | copy-start | bytes 11010052
  528.8 85.1 %copy-start.3 = (bf16[512,4096]{1,0:T(8,128)(2,1)S(1)}, bf16[512,4096]{1,0:T(8,128)(2,1)}, u32[]{:S(2)}) copy-start(bf16[512,4096]{1,0:T(8,128)(2,1)} %all-gather.2.cloned.1.call-done) | copy-start | bytes 12582916
Sparse Core Ops, SparseCore 0:
  10.0 75.1 all-gather.1
  636.9 73.4 reduce-scatter.1
where the time goes:
time: 743 us; the launch traced here: 734 us
  blocking collectives  340 us (46%)
  waiting for transfers between devices  152 us (20%)
  matrix products  105 us (14%)
  local copies, waits for them, and re-layouts  67.3 us (9%)
  other arithmetic  55.2 us (7%)
  between operations  14.6 us (2%)
    all_to_all x1, blocking collectives, per_device(): lax.all_to_all(quant_rows, 'tensor', split_axis=1, concat_axis=0, tiled=T...  85.1 us
    all_to_all x1, blocking collectives, per_device(): lax.all_to_all(back_rows, 'tensor', split_axis=1, concat_axis=0, tiled=True)  85.1 us
    all_to_all x1, blocking collectives, per_device(): lax.all_to_all(hidden, 'tensor', split_axis=0, concat_axis=1, tiled=True)  85 us
    all_to_all x1, blocking collectives, per_device(): lax.all_to_all(rot_grad, 'tensor', split_axis=0, concat_axis=1, tiled=True)  84.9 us
    all_gather x1, waiting for transfers between devices, per_device(): full_grad = lax.all_gather(out_grad, 'tensor', axis=1, tiled=True)  77.3 us
    reduce_scatter x1, waiting for transfers between devices, per_device(): lax.psum_scatter(partial_grad, 'dp', scatter_dimension=1, tiled=True)  73.7 us
    dot_general x2, matrix products, rotate(): jnp.einsum('ac,tad->tcd', small_table, first_section, precision=lax.Preci...  33 us
    convert_element_type x1, other arithmetic, quantize(): return (staircase * spacing).reshape(rotated.shape).astype(jnp.bfloat16)  27 us
  transfers between devices with their start and end apart: 2, of which 2 were waited for; matrix products, arithmetic and copies ran while one was open for 0% of the time, Pallas kernels for 0%

commit v1 on v0

--- a/solution.py
+++ b/solution.py
@@ -1,13 +1,20 @@
+import functools
 import math
 
 import jax
 import jax.numpy as jnp
 import numpy as np
 from jax import lax
+from jax.experimental import pallas as pl
+from jax.experimental.pallas import tpu as pltpu
 from jax.sharding import PartitionSpec as P
 
 HAD_LARGE = 1024
 GROUP = 128
+PIECE = 512
+MESH = pl.DeviceIdType.MESH
+ANY = pl.BlockSpec(memory_space=pl.ANY)
+VMEM_LIMIT = 56 * 1024 * 1024
 
 
 def paley_table():
@@ -89,9 +96,351 @@
     return (grad_gate, grad_up, grad_down)
 
 
+def conference():
+    signs = paley_table()[::2, ::2].copy()
+    np.fill_diagonal(signs, 0.0)
+    return signs
+
+
+SINE = tuple((0.9999999944722885, -6.579735439437039, 12.987842893122675, -12.207428862951517, 6.6870661467168215, -2.3663670610371574, 0.5091905912043592))
+
+
+def greet(n, sibling=False):
+    me = lax.axis_index("tensor")
+    barrier = pltpu.get_barrier_semaphore()
+    for step in range(1, n):
+        pl.semaphore_signal(
+            barrier, inc=1, device_id={"tensor": lax.rem(me + step, n)}, device_id_type=MESH
+        )
+    if sibling:
+        other = 1 - lax.axis_index("dp")
+        pl.semaphore_signal(barrier, inc=1, device_id={"dp": other}, device_id_type=MESH)
+    pl.semaphore_wait(barrier, n if sibling else n - 1)
+
+
+def start_exchange(n, source, target, send, recv, own):
+    me = lax.axis_index("tensor")
+    pending = []
+    for step in sorted(range(1, n), key=lambda s: abs(s - n // 2)):
+        peer = lax.rem(me + step, n)
+        copy = pltpu.make_async_remote_copy(
+            src_ref=source.at[peer],
+            dst_ref=target.at[me],
+            send_sem=send.at[step],
+            recv_sem=recv.at[step],
+            device_id={"tensor": peer},
+            device_id_type=MESH,
+        )
+        copy.start()
+        pending.append(copy)
+    local = pltpu.make_async_copy(source.at[me], target.at[me], own)
+    local.start()
+    pending.append(local)
+    return pending
+
+
+def forward_kernel(
+    n, hidden, out_grad, weight, full_grad, token_hidden, rot_grad,
+    weight_v, grad_v, rot_v, send, recv, own, gather_send, gather_recv, local_sem, weight_sem,
+):
+    me = lax.axis_index("tensor")
+    pairs = n // 2
+    row, side = me // 2, lax.rem(me, 2)
+    width = out_grad.shape[1]
+    load_weight = pltpu.make_async_copy(weight, weight_v, weight_sem)
+    load_weight.start()
+    greet(n)
+    partner = row * 2 + 1 - side
+
+    def push(source, slot, peer, at):
+        return pltpu.make_async_remote_copy(
+            src_ref=source,
+            dst_ref=full_grad.at[slot],
+            send_sem=gather_send.at[at],
+            recv_sem=gather_recv.at[at],
+            device_id={"tensor": peer},
+            device_id_type=MESH,
+        )
+
+    def stage(slot, source, at):
+        columns = pl.ds(pl.multiple_of(slot * width, width), width)
+        copy = pltpu.make_async_copy(source, grad_v.at[:, columns], local_sem.at[at])
+        copy.start()
+        return copy
+
+    first = []
+    for step in range(1, pairs):
+        copy = push(out_grad, me, lax.rem(row + step, pairs) * 2 + side, step)
+        copy.start()
+        first.append(copy)
+    across = push(out_grad, me, partner, 0)
+    across.start()
+    own_grad = pltpu.make_async_copy(out_grad, full_grad.at[me], local_sem.at[n])
+    own_grad.start()
+    staged = [stage(me, out_grad, 0)]
+    passed = []
+    for step in range(1, pairs):
+        first[step - 1].wait_recv()
+        slot = lax.rem(row + pairs - step, pairs) * 2 + side
+        copy = push(full_grad.at[slot], slot, partner, pairs + step)
+        copy.start()
+        passed.append(copy)
+        staged.append(stage(slot, full_grad.at[slot], step))
+    pending = start_exchange(n, hidden, token_hidden, send, recv, own)
+    across.wait_recv()
+    staged.append(stage(partner, full_grad.at[partner], pairs))
+    for step in range(1, pairs):
+        passed[step - 1].wait_recv()
+        slot = lax.rem(row + pairs - step, pairs) * 2 + 1 - side
+        staged.append(stage(slot, full_grad.at[slot], pairs + step))
+    for copy in staged:
+        copy.wait()
+    load_weight.wait()
+
+    @pl.loop(0, weight.shape[0] // 256)
+    def _(tile):
+        rows = pl.ds(pl.multiple_of(tile * 256, 256), 256)
+        rot_v[:, rows] = lax.dot_general(
+            grad_v[...], weight_v[rows, :], (((1,), (1,)), ((), ())),
+            preferred_element_type=jnp.float32,
+        ).astype(rot_v.dtype)
+
+    store = pltpu.make_async_copy(rot_v, rot_grad, weight_sem)
+    store.start()
+    store.wait()
+    own_grad.wait()
+    for copy in first + passed + [across]:
+        copy.wait_send()
+    for copy in pending:
+        copy.wait()
+
+
+def round_levels(value):
+    largest = jnp.max(jnp.abs(value), axis=-1, keepdims=True)
+    spacing = largest * (0.9 / 7.0) + 1e-06
+    scaled = value * (1.0 / spacing)
+    rest = scaled - jnp.round(scaled)
+    square = rest * rest
+    wave = jnp.full_like(square, SINE[-1])
+    for factor in SINE[-2::-1]:
+        wave = wave * square + factor
+    return jnp.minimum(scaled - wave * rest, 7.0) * spacing
+
+
+def rotate_kernel(
+    n, quantized, rows_in, table, outgoing, rows_out, incoming,
+    in_v, table_v, mid_v, out_v, send, recv, own, local_sem,
+):
+    load = pltpu.make_async_copy(rows_in, in_v, local_sem.at[0])
+    load.start()
+    load_table = pltpu.make_async_copy(table, table_v, local_sem.at[1])
+    load_table.start()
+    greet(n)
+    pending = start_exchange(n, outgoing, incoming, send, recv, own)
+    load.wait()
+    load_table.wait()
+    tokens = rows_in.shape[1]
+    per = rows_in.shape[2] // PIECE
+    scale = 1.0 / math.sqrt(n * per * PIECE)
+
+    @pl.loop(0, n)
+    def _(at):
+        block = in_v[at]
+        stacked = jnp.concatenate(
+            [block[:, PIECE * k : PIECE * (k + 1)] for k in range(per)], axis=0
+        )
+        first = jnp.dot(stacked, table_v[...], preferred_element_type=jnp.float32)
+        mid_v[pl.ds(at * per, per)] = first.reshape(per, tokens, PIECE)
+
+    signs = conference()
+    order = signs.shape[0]
+    lane_tiles = PIECE // GROUP
+
+    @pl.loop(0, tokens // 16 * lane_tiles)
+    def _(step):
+        rows = pl.ds(pl.multiple_of((step // lane_tiles) * 16, 16), 16)
+        lane = (step % lane_tiles) * GROUP
+        lanes = pl.ds(pl.multiple_of(lane, GROUP), GROUP)
+
+        def total(i, j, half):
+            even, odd = mid_v[i * 4 + j * 2, rows, lanes], mid_v[i * 4 + j * 2 + 1, rows, lanes]
+            return even - odd if half else even + odd
+
+        for half in range(2):
+            mixed = [[None] * order, [None] * order]
+            for i in range(order):
+                one, two = total(i, 0, half), total(i, 1, half)
+                mixed[0][i] = one + two
+                mixed[1][i] = one - two
+            for j in range(2):
+                for i in range(order):
+                    value = mixed[1][i] if j == 0 else -mixed[0][i]
+                    for other in range(order):
+                        if signs[other, i] > 0:
+                            value = value + mixed[j][other]
+                        elif signs[other, i] < 0:
+                            value = value - mixed[j][other]
+                    value = value * scale
+                    if quantized:
+                        value = round_levels(value)
+                    unit = i * 4 + j * 2 + half
+                    place = pl.ds(pl.multiple_of(lane + unit % per * PIECE, GROUP), GROUP)
+                    out_v[unit // per, rows, place] = value.astype(out_v.dtype)
+
+    store = pltpu.make_async_copy(out_v, rows_out, local_sem.at[0])
+    store.start()
+    store.wait()
+    for copy in pending:
+        copy.wait()
+
+
+def gradient_kernel(
+    n, quantized, full_grad, outgoing, grad_down, incoming,
+    quant_v, grad_v, down_v, send, recv, own, side_send, side_recv, local_sem,
+):
+    core = lax.axis_index("dp")
+    other = 1 - core
+    half = n // 2
+    tokens = full_grad.shape[1]
+    width = full_grad.shape[2]
+
+    def columns(which):
+        return full_grad.at[pl.ds(which * half, half)]
+
+    loads = [
+        pltpu.make_async_copy(quantized, quant_v.at[pl.ds(0, n)], local_sem.at[0]),
+        pltpu.make_async_copy(columns(core), grad_v.at[0], local_sem.at[1]),
+    ]
+    for copy in loads:
+        copy.start()
+    greet(n, sibling=True)
+    shared = []
+    for at, (source, target) in enumerate(
+        [(quantized, quant_v.at[pl.ds(n, n)]), (columns(other), grad_v.at[1])]
+    ):
+        copy = pltpu.make_async_remote_copy(
+            src_ref=source,
+            dst_ref=target,
+            send_sem=side_send.at[at],
+            recv_sem=side_recv.at[at],
+            device_id={"dp": other},
+            device_id_type=MESH,
+        )
+        copy.start()
+        shared.append(copy)
+    pending = start_exchange(n, outgoing, incoming, send, recv, own)
+    for copy in loads + shared:
+        copy.wait()
+
+    @pl.loop(0, grad_down.shape[0] // 256)
+    def _(tile):
+        units = pl.ds(pl.multiple_of(tile * 256, 256), 256)
+        levels = quant_v[:, :, units].reshape(2, tokens, 256)
+        mine, theirs = levels[0].T, levels[1].T
+        for at in range(half):
+            total = jnp.dot(mine, grad_v[0, at], preferred_element_type=jnp.float32)
+            total += jnp.dot(theirs, grad_v[1, at], preferred_element_type=jnp.float32)
+            down_v[units, at * width : (at + 1) * width] = total.astype(down_v.dtype)
+
+    store = pltpu.make_async_copy(down_v, grad_down, local_sem.at[0])
+    store.start()
+    store.wait()
+    for copy in pending:
+        copy.wait()
+
+
+def call(kernel, outs, scratch, number, flops, operands):
+    dma = pltpu.SemaphoreType.DMA
+    return pl.pallas_call(
+        kernel,
+        out_shape=[jax.ShapeDtypeStruct(shape, jnp.bfloat16) for shape in outs],
+        in_specs=[ANY] * len(operands),
+        out_specs=[ANY] * len(outs),
+        scratch_shapes=[dma(s) if isinstance(s, tuple) else s for s in scratch],
+        compiler_params=pltpu.CompilerParams(
+            collective_id=number, has_side_effects=True, vmem_limit_bytes=VMEM_LIMIT
+        ),
+        cost_estimate=pl.CostEstimate(flops=flops, bytes_accessed=40_000_000, transcendentals=0),
+    )(*operands)
+
+
+def with_kernels(n, gate_pre, up_pre, down_weight, out_grad):
+    tokens, units = gate_pre.shape
+    width, part = out_grad.shape[1], tokens // n
+    features = n * width
+    per = units // PIECE
+    gate_wide = gate_pre.astype(jnp.float32)
+    up_wide = up_pre.astype(jnp.float32)
+    sigmoid_gate = jax.nn.sigmoid(gate_wide)
+    activated = gate_wide * sigmoid_gate
+    hidden = (activated * up_wide).astype(jnp.bfloat16).reshape(n, part, units)
+    table = sylvester(PIECE).astype(jnp.bfloat16)
+    blocks = (n, part, units)
+    wide, one = jnp.bfloat16, ()
+    exchange = [(n,), (n,), one]
+
+    full_grad, token_hidden, rot_grad = call(
+        functools.partial(forward_kernel, n),
+        [(n, tokens, width), blocks, (tokens, units)],
+        [
+            pltpu.VMEM((units, features), wide),
+            pltpu.VMEM((tokens, features), wide),
+            pltpu.VMEM((tokens, units), wide),
+            *exchange, (n,), (n,), (n + 1,), one,
+        ],
+        1, 2 * tokens * units * features, [hidden, out_grad, down_weight],
+    )
+
+    def rotated(rows_in, outgoing, quantized, number):
+        return call(
+            functools.partial(rotate_kernel, n, quantized),
+            [blocks, blocks],
+            [
+                pltpu.VMEM(blocks, wide),
+                pltpu.VMEM((PIECE, PIECE), wide),
+                pltpu.VMEM((n * per, part, PIECE), jnp.float32),
+                pltpu.VMEM(blocks, wide),
+                *exchange, (2,),
+            ],
+            number, 2 * part * n * units * PIECE, [rows_in, table, outgoing],
+        )
+
+    quant_rows, token_grad = rotated(token_hidden, rot_grad.reshape(blocks), True, 2)
+    back_rows, quantized = rotated(token_grad, quant_rows, False, 3)
+    grad_down, hidden_grad = call(
+        functools.partial(gradient_kernel, n),
+        [(units, features // 2), blocks],
+        [
+            pltpu.VMEM((2 * n, part, units), wide),
+            pltpu.VMEM((2, n // 2, tokens, width), wide),
+            pltpu.VMEM((units, features // 2), wide),
+            *exchange, (2,), (2,), (2,),
+        ],
+        4, 2 * tokens * units * features, [quantized, full_grad, back_rows],
+    )
+    hid_wide = hidden_grad.reshape(tokens, units).astype(jnp.float32)
+    grad_up = (hid_wide * activated).astype(jnp.bfloat16)
+    grad_gate = (
+        hid_wide * up_wide * sigmoid_gate * (1.0 + gate_wide * (1.0 - sigmoid_gate))
+    ).astype(jnp.bfloat16)
+    return (grad_gate, grad_up, grad_down)
+
+
+def choose(n, cores, gate_pre, up_pre, down_weight, out_grad):
+    tokens, units = gate_pre.shape
+    fits = (
+        n % 2 == 0 and n <= 16 and cores == 2
+        and tokens % (16 * n) == 0 and units % PIECE == 0 and units % 256 == 0
+        and n * units == 28 * HAD_LARGE and out_grad.shape[1] % 128 == 0
+    )
+    if fits:
+        return with_kernels(n, gate_pre, up_pre, down_weight, out_grad)
+    return per_device(gate_pre, up_pre, down_weight, out_grad)
+
+
 def solution(mesh):
     return jax.shard_map(
-        per_device,
+        functools.partial(choose, mesh.shape["tensor"], mesh.shape["dp"]),
         mesh=mesh,
         in_specs=(
             P(("groups", "dp"), "tensor"),

time: 743 us -> 410 us (0.55); the launches traced: 734 us -> 409 us
  Pallas kernels: 0 us -> 387 us
  blocking collectives: 340 us -> 0 us
  waiting for transfers between devices: 152 us -> 0 us
  matrix products: 105 us -> 0 us
  local copies, waits for them, and re-layouts: 67.3 us -> 6.94 us
  other arithmetic: 55.2 us -> 15.2 us
  between operations: 14.6 us -> 0.7 us
    pallas_call x0 -> x4, Pallas kernels: none -> 387 us  [call(): pl.pallas_call(kernel, out_shape=[jax.ShapeDtypeStruct(shape, jnp.bfloat1...]
    all_to_all x4 -> x0, blocking collectives: 340 us -> none  [the longest x1 85.1 us: per_device(): lax.all_to_all(quant_rows, 'tensor', split_axis=1, concat_axis=0, tiled=T...]
    dot_general x6 -> x0, matrix products: 105 us -> none  [the longest x2 33 us: rotate(): jnp.einsum('ac,tad->tcd', small_table, first_section, precision=lax.Preci...]
    all_gather x1 -> x0, waiting for transfers between devices: 77.3 us -> none  [per_device(): full_grad = lax.all_gather(out_grad, 'tensor', axis=1, tiled=True)]
    reduce_scatter x1 -> x0, waiting for transfers between devices: 73.7 us -> none  [per_device(): lax.psum_scatter(partial_grad, 'dp', scatter_dimension=1, tiled=True)]
    convert_element_type x3, other arithmetic: 49.8 us -> 15.2 us  [the longest x1 7.45 us: with_kernels(): grad_up = (hid_wide * activated).astype(jnp.bfloat16)]
    dot_general x2 -> x0, local copies, waits for them, and re-layouts: 16 us -> none  [rotate(): jnp.dot(rows_in.reshape(row_count * small_order, large_order), large_tabl...]
    div x2 -> x0, local copies, waits for them, and re-layouts: 12.5 us -> none  [quantize(): scaled = grouped / spacing]
  transfers between devices with their start and end apart: 2 -> 0, of which waited for: 2 -> 0; matrix products, arithmetic and copies ran while one was open for 0% -> 0% of each run, Pallas kernels for 0% -> 0%
where the time goes in v1:
time: 410 us; the launch traced here: 409 us
  Pallas kernels  387 us (94%)
  other arithmetic  15.2 us (4%)
  local copies, waits for them, and re-layouts  6.94 us (2%)
    pallas_call x4, Pallas kernels, call(): pl.pallas_call(kernel, out_shape=[jax.ShapeDtypeStruct(shape, jnp.bfloat1...  387 us

profile of v1, /device:TPU:16, one launch (start us, length us, event | category | flops | bytes accessed | tf_op | source)
XLA Modules:
  0.0 409.5 jit_solution(2045331555242159029)
XLA Ops:
  0.6 5.5 %fusion = bf16[512,3584]{1,0:T(8,128)(2,1)} fusion(bf16[512,3584]{1,0:T(8,128)(2,1)} %param.5, bf16[512,3584]{1,0:T(8,128)(2,1)} %param.4), kind=kLoop, calls=%fused_computation.6 | loop fusion | flops 14680064 | bytes 11010048 | tf_op jit(solution)/shard_map/convert_element_type | solution.py:376
  6.1 128.7 %shard_map.67 = (bf16[8,512,512]{2,1,0:T(8,128)(2,1)}, bf16[8,64,3584]{2,1,0:T(8,128)(2,1)}, bf16[512,3584]{1,0:T(8,128)(2,1)}) custom-call(bf16[8,64,3584]{2,1,0:T(8,128)(2,1)} %bitcast.7, bf16[512,512]{1,0:T(8,128)(2,1)} %out_grad.1, bf16[3584,4096]{1,0:T(8,128)(2,1)} %weight.1), custom_call_target="tpu_custom_call" | custom-call | flops 15032385536 | bytes 40000000 | tf_op jit(solution)/shard_map/pallas_call | solution.py:354
  134.8 2.2 fusion.13.table
  137.1 93.2 %shard_map.68 = (bf16[8,64,3584]{2,1,0:T(8,128)(2,1)}, bf16[8,64,3584]{2,1,0:T(8,128)(2,1)}) custom-call(bf16[8,64,3584]{2,1,0:T(8,128)(2,1)} %get-tuple-element.12.rows_in, bf16[512,512]{1,0:T(8,128)(2,1)} %fusion.13.table, bf16[8,64,3584]{2,1,0:T(8,128)(2,1)} %bitcast.6), custom_call_target="tpu_custom_call" | custom-call | flops 1879048192 | bytes 40000000 | tf_op jit(solution)/shard_map/pallas_call | solution.py:354
  230.3 82.8 %shard_map.69 = (bf16[8,64,3584]{2,1,0:T(8,128)(2,1)}, bf16[8,64,3584]{2,1,0:T(8,128)(2,1)}) custom-call(bf16[8,64,3584]{2,1,0:T(8,128)(2,1)} %get-tuple-element.14.rows_in, bf16[512,512]{1,0:T(8,128)(2,1)} %fusion.13.table, bf16[8,64,3584]{2,1,0:T(8,128)(2,1)} %get-tuple-element.15.outgoing), custom_call_target="tpu_custom_call" | custom-call | flops 1879048192 | bytes 40000000 | tf_op jit(solution)/shard_map/pallas_call | solution.py:354
  313.1 0.0 copy-start.1
  313.1 0.0 copy-start.2
  313.1 82.0 %shard_map.70 = (bf16[3584,2048]{1,0:T(8,128)(2,1)}, bf16[8,64,3584]{2,1,0:T(8,128)(2,1)}) custom-call(bf16[8,64,3584]{2,1,0:T(8,128)(2,1)} %get-tuple-element.16.quantized, bf16[8,512,512]{2,1,0:T(8,128)(2,1)} %get-tuple-element.17.full_grad, bf16[8,64,3584]{2,1,0:T(8,128)(2,1)} %get-tuple-element.18.outgoing), custom_call_target="tpu_custom_call" | custom-call | flops 15032385536 | bytes 40000000 | tf_op jit(solution)/shard_map/pallas_call | solution.py:354
  395.1 0.0 copy-done.1
  395.1 0.0 copy-done.2
  395.1 0.0 copy-start
  395.1 7.5 %fusion.4 = (bf16[512,3584]{1,0:T(8,128)(2,1)}, bf16[512,3584]{1,0:T(8,128)(2,1)}) fusion(bf16[8,64,3584]{2,1,0:T(8,128)(2,1)} %get-tuple-element.19, bf16[512,3584]{1,0:T(8,128)(2,1)S(1)} %copy-done.2, bf16[512,3584]{1,0:T(8,128)(2,1)S(1)} %copy-done.1), kind=kLoop, calls=%fused_computation.10 | loop fusion | flops 29360128 | bytes 18350080 | tf_op jit(solution)/shard_map/convert_element_type | solution.py:422
  402.6 1.5 copy-done
  404.0 5.5 %copy.8 = bf16[3584,2048]{1,0:T(8,128)(2,1)} copy(bf16[3584,2048]{1,0:T(8,128)(2,1)S(1)} %copy-done) | data formatting | bytes 29360128
Async XLA Ops:
  313.1 82.0 %copy-start.1 = (bf16[512,3584]{1,0:T(8,128)(2,1)S(1)}, bf16[512,3584]{1,0:T(8,128)(2,1)}, u32[]{:S(2)}) copy-start(bf16[512,3584]{1,0:T(8,128)(2,1)} %param.5) | copy-start | bytes 11010052
  313.1 82.0 %copy-start.2 = (bf16[512,3584]{1,0:T(8,128)(2,1)S(1)}, bf16[512,3584]{1,0:T(8,128)(2,1)}, u32[]{:S(2)}) copy-start(bf16[512,3584]{1,0:T(8,128)(2,1)} %param.4) | copy-start | bytes 11010052
  395.1 8.9 %copy-start = (bf16[3584,2048]{1,0:T(8,128)(2,1)S(1)}, bf16[3584,2048]{1,0:T(8,128)(2,1)}, u32[]{:S(2)}) copy-start(bf16[3584,2048]{1,0:T(8,128)(2,1)} %get-tuple-element.28) | copy-start | bytes 44040196

commit v2 on v0

--- a/solution.py
+++ b/solution.py
@@ -1,13 +1,20 @@
+import functools
 import math
 
 import jax
 import jax.numpy as jnp
 import numpy as np
 from jax import lax
+from jax.experimental import pallas as pl
+from jax.experimental.pallas import tpu as pltpu
 from jax.sharding import PartitionSpec as P
 
 HAD_LARGE = 1024
 GROUP = 128
+PIECE = 512
+MESH = pl.DeviceIdType.MESH
+ANY = pl.BlockSpec(memory_space=pl.ANY)
+VMEM_LIMIT = 60 * 1024 * 1024
 
 
 def paley_table():
@@ -89,9 +96,358 @@
     return (grad_gate, grad_up, grad_down)
 
 
+def conference():
+    signs = paley_table()[::2, ::2].copy()
+    np.fill_diagonal(signs, 0.0)
+    return signs
+
+
+SINE = tuple((0.9999999944722885, -6.579735439437039, 12.987842893122675, -12.207428862951517, 6.6870661467168215, -2.3663670610371574, 0.5091905912043592))
+
+
+def greet(n, sibling=False):
+    me = lax.axis_index("tensor")
+    barrier = pltpu.get_barrier_semaphore()
+    for step in range(1, n):
+        pl.semaphore_signal(
+            barrier, inc=1, device_id={"tensor": lax.rem(me + step, n)}, device_id_type=MESH
+        )
+    if sibling:
+        other = 1 - lax.axis_index("dp")
+        pl.semaphore_signal(barrier, inc=1, device_id={"dp": other}, device_id_type=MESH)
+    pl.semaphore_wait(barrier, n if sibling else n - 1)
+
+
+def round_levels(value):
+    largest = jnp.max(jnp.abs(value), axis=-1, keepdims=True)
+    spacing = largest * (0.9 / 7.0) + 1e-06
+    scaled = value * (1.0 / spacing)
+    rest = scaled - jnp.round(scaled)
+    square = rest * rest
+    wave = jnp.full_like(square, SINE[-1])
+    for factor in SINE[-2::-1]:
+        wave = wave * square + factor
+    return jnp.minimum(scaled - wave * rest, 7.0) * spacing
+
+
+def exchange(n, source, target, send, recv):
+    me = lax.axis_index("tensor")
+    copies = []
+    for step in sorted(range(1, n), key=lambda s: abs(s - n // 2)):
+        peer = lax.rem(me + step, n)
+        copy = pltpu.make_async_remote_copy(
+            src_ref=source.at[peer],
+            dst_ref=target.at[me],
+            send_sem=send.at[step],
+            recv_sem=recv.at[step],
+            device_id={"tensor": peer},
+            device_id_type=MESH,
+        )
+        copy.start()
+        copies.append(copy)
+    local = pltpu.make_async_copy(source.at[me], target.at[me], recv.at[0])
+    local.start()
+    return copies, local
+
+
+def arrived(pending):
+    for copy in pending[0]:
+        copy.wait_recv()
+    pending[1].wait()
+
+
+def gather_columns(n, out_grad, grad_v, sems, between):
+    me = lax.axis_index("tensor")
+    line = n // 2
+    width = out_grad.shape[1]
+    row, side = me // 2, lax.rem(me, 2)
+
+    def slot(at_row, at_side):
+        place = lax.rem(at_row + line, line) * 2 + at_side
+        return grad_v.at[:, pl.ds(pl.multiple_of(place * width, width), width)]
+
+    def push(source_row, peer, at):
+        return pltpu.make_async_remote_copy(
+            src_ref=slot(source_row, side),
+            dst_ref=slot(source_row, side),
+            send_sem=sems.at[0, at],
+            recv_sem=sems.at[1, at],
+            device_id={"tensor": peer},
+            device_id_type=MESH,
+        )
+
+    def along(sign, hop):
+        peer = lax.rem(row + sign + line, line) * 2 + side
+        return push(row - sign * (hop - 1), peer, hop if sign > 0 else line + hop)
+
+    def across(sign, hop):
+        at = 2 * line + (0 if hop == 0 else hop if sign > 0 else line + hop)
+        return push(row - sign * hop, row * 2 + 1 - side, at)
+
+    def has(sign, hop):
+        return row - hop >= 0 if sign > 0 else row + hop < line
+
+    for sign in (1, -1):
+        pl.when(has(-sign, 1))(lambda sign=sign: along(sign, 1).start())
+    across(1, 0).start()
+    for hop in range(1, line):
+        for sign in (1, -1):
+
+            @pl.when(has(sign, hop))
+            def _(sign=sign, hop=hop):
+                along(sign, hop).wait_recv()
+                if hop + 1 < line:
+                    pl.when(has(-sign, 1))(lambda: along(sign, hop + 1).start())
+                across(sign, hop).start()
+
+        if hop == 1:
+            pending = between()
+    across(1, 0).wait()
+    for hop in range(1, line):
+        for sign in (1, -1):
+
+            @pl.when(has(sign, hop))
+            def _(sign=sign, hop=hop):
+                across(sign, hop).wait()
+
+            @pl.when(has(sign, hop - 1) & has(-sign, 1))
+            def _(sign=sign, hop=hop):
+                along(sign, hop).wait_send()
+
+    return pending
+
+
+def rotate_pieces(n, quantized, in_v, table_v, mid_v, out_v):
+    tokens = in_v.shape[1]
+    per = in_v.shape[2] // PIECE
+    scale = 1.0 / math.sqrt(n * per * PIECE)
+
+    @pl.loop(0, n)
+    def _(at):
+        block = in_v[at]
+        stacked = jnp.concatenate(
+            [block[:, PIECE * k : PIECE * (k + 1)] for k in range(per)], axis=0
+        )
+        first = jnp.dot(stacked, table_v[...], preferred_element_type=jnp.float32)
+        mid_v[pl.ds(at * per, per)] = first.reshape(per, tokens, PIECE)
+
+    signs = conference()
+    order = signs.shape[0]
+    lane_tiles = PIECE // GROUP
+
+    @pl.loop(0, tokens // 16 * lane_tiles)
+    def _(step):
+        rows = pl.ds(pl.multiple_of((step // lane_tiles) * 16, 16), 16)
+        lane = (step % lane_tiles) * GROUP
+        lanes = pl.ds(pl.multiple_of(lane, GROUP), GROUP)
+
+        def total(i, j, half):
+            even, odd = mid_v[i * 4 + j * 2, rows, lanes], mid_v[i * 4 + j * 2 + 1, rows, lanes]
+            return even - odd if half else even + odd
+
+        for half in range(2):
+            mixed = [[None] * order, [None] * order]
+            for i in range(order):
+                one, two = total(i, 0, half), total(i, 1, half)
+                mixed[0][i] = one + two
+                mixed[1][i] = one - two
+            for j in range(2):
+                for i in range(order):
+                    value = mixed[1][i] if j == 0 else -mixed[0][i]
+                    for other in range(order):
+                        if signs[other, i] > 0:
+                            value = value + mixed[j][other]
+                        elif signs[other, i] < 0:
+                            value = value - mixed[j][other]
+                    value = value * scale
+                    if quantized:
+                        value = round_levels(value)
+                    unit = i * 4 + j * 2 + half
+                    place = pl.ds(pl.multiple_of(lane + unit % per * PIECE, GROUP), GROUP)
+                    out_v[unit // per, rows, place] = value.astype(out_v.dtype)
+
+
+def whole_kernel(
+    n, gate, up, out_grad, weight, table, hidden_grad, grad_down,
+    hidden_v, token_v, rot_v, back_in_v, mid_v, out_v, back_v, quant_v,
+    grad_v, side_grad_v, weight_v, down_v, table_v,
+    gather_sem, send, recv, side_send, side_recv, local_sem, weight_sem, down_sem,
+):
+    me = lax.axis_index("tensor")
+    core = lax.axis_index("dp")
+    tokens, width = out_grad.shape
+    part = tokens // n
+    features = n * width
+    half = features // 2
+    tiles = weight.shape[0] // 256
+    mine = pl.ds(pl.multiple_of(me * width, width), width)
+    loads = [
+        pltpu.make_async_copy(source, target, local_sem.at[at])
+        for at, (source, target) in enumerate(
+            [(gate, out_v), (up, back_v), (table, table_v), (out_grad, grad_v.at[:, mine])]
+        )
+    ]
+    for copy in loads:
+        copy.start()
+
+    def fetch(tile):
+        slot = lax.rem(tile, 2)
+        rows = pl.ds(pl.multiple_of(tile * 256, 256), 256)
+        return pltpu.make_async_copy(weight.at[rows], weight_v.at[slot], weight_sem.at[slot])
+
+    fetch(0).start()
+    greet(n, sibling=True)
+    loads[3].wait()
+
+    def make_hidden():
+        loads[0].wait()
+        loads[1].wait()
+
+        @pl.loop(0, n * part // 16)
+        def _(step):
+            at = step // (part // 16)
+            rows = pl.ds(pl.multiple_of(step % (part // 16) * 16, 16), 16)
+            wide = out_v[at, rows, :].astype(jnp.float32)
+            active = wide * jax.nn.sigmoid(wide)
+            hidden_v[at, rows, :] = (active * back_v[at, rows, :].astype(jnp.float32)).astype(
+                hidden_v.dtype
+            )
+
+        return exchange(n, hidden_v, token_v, send.at[0], recv.at[0])
+
+    to_tokens = gather_columns(n, out_grad, grad_v, gather_sem, make_hidden)
+
+    @pl.loop(0, tiles)
+    def _(tile):
+        pl.when(tile + 1 < tiles)(lambda: fetch(tile + 1).start())
+        fetch(tile).wait()
+        units = pl.ds(pl.multiple_of(tile * 256, 256), 256)
+        product = lax.dot_general(
+            grad_v[...], weight_v[lax.rem(tile, 2)], (((1,), (1,)), ((), ())),
+            preferred_element_type=jnp.float32,
+        )
+        rot_v[:, :, units] = product.astype(rot_v.dtype).reshape(n, part, 256)
+
+    grads_to_tokens = exchange(n, rot_v, back_in_v, send.at[1], recv.at[1])
+
+    def beside(which):
+        return grad_v.at[:, pl.ds(pl.multiple_of(which * half, half), half)]
+
+    def to_sibling(source, target, at):
+        copy = pltpu.make_async_remote_copy(
+            src_ref=source,
+            dst_ref=target,
+            send_sem=side_send.at[at],
+            recv_sem=side_recv.at[at],
+            device_id={"dp": 1 - core},
+            device_id_type=MESH,
+        )
+        copy.start()
+        return copy
+
+    side_grad = to_sibling(beside(1 - core), side_grad_v, 0)
+    loads[2].wait()
+    arrived(to_tokens)
+    rotate_pieces(n, True, token_v, table_v, mid_v, out_v)
+    own_levels = quant_v.at[pl.ds(0, n)]
+    levels = exchange(n, out_v, own_levels, send.at[2], recv.at[2])
+    arrived(grads_to_tokens)
+    rotate_pieces(n, False, back_in_v, table_v, mid_v, back_v)
+    grads_back = exchange(n, back_v, hidden_grad, send.at[3], recv.at[3])
+    arrived(levels)
+    side_levels = to_sibling(own_levels, quant_v.at[pl.ds(n, n)], 1)
+    side_grad.wait()
+    side_levels.wait()
+
+    def write(tile):
+        slot = lax.rem(tile, 2)
+        rows = pl.ds(pl.multiple_of(tile * 256, 256), 256)
+        return pltpu.make_async_copy(down_v.at[slot], grad_down.at[rows], down_sem.at[slot])
+
+    own_columns = pl.ds(pl.multiple_of(core * half, half), half)
+
+    @pl.loop(0, tiles)
+    def _(tile):
+        pl.when(tile >= 2)(lambda: write(tile - 2).wait())
+        units = pl.ds(pl.multiple_of(tile * 256, 256), 256)
+        rows = quant_v[:, :, units].reshape(2, tokens, 256)
+        total = jnp.dot(rows[0].T, grad_v[:, own_columns], preferred_element_type=jnp.float32)
+        total += jnp.dot(rows[1].T, side_grad_v[...], preferred_element_type=jnp.float32)
+        down_v[lax.rem(tile, 2)] = total.astype(down_v.dtype)
+        write(tile).start()
+
+    for tile in range(max(tiles - 2, 0), tiles):
+        write(tile).wait()
+    arrived(grads_back)
+    for copies, _ in (to_tokens, grads_to_tokens, levels, grads_back):
+        for copy in copies:
+            copy.wait_send()
+
+
+def with_kernel(n, gate_pre, up_pre, down_weight, out_grad):
+    tokens, units = gate_pre.shape
+    width, part = out_grad.shape[1], tokens // n
+    features = n * width
+    blocks = (n, part, units)
+    wide = jnp.bfloat16
+    table = jnp.asarray(functools.reduce(np.kron, [[[1.0, 1.0], [1.0, -1.0]]] * (PIECE.bit_length() - 1)), wide)
+    dma = pltpu.SemaphoreType.DMA
+    keep = pltpu.VMEM(blocks, wide)
+    hidden_grad, grad_down = pl.pallas_call(
+        functools.partial(whole_kernel, n),
+        out_shape=[
+            jax.ShapeDtypeStruct(blocks, wide),
+            jax.ShapeDtypeStruct((units, features // 2), wide),
+        ],
+        in_specs=[ANY] * 5,
+        out_specs=[ANY] * 2,
+        scratch_shapes=[
+            keep, keep, keep, keep,
+            pltpu.VMEM((n * units // PIECE, part, PIECE), jnp.float32),
+            keep, keep,
+            pltpu.VMEM((2 * n, part, units), wide),
+            pltpu.VMEM((tokens, features), wide),
+            pltpu.VMEM((tokens, features // 2), wide),
+            pltpu.VMEM((2, 256, features), wide),
+            pltpu.VMEM((2, 256, features // 2), wide),
+            pltpu.VMEM((PIECE, PIECE), wide),
+            dma((2, 2 * n)), dma((4, n)), dma((4, n)), dma((2,)), dma((2,)),
+            dma((4,)), dma((2,)), dma((2,)),
+        ],
+        compiler_params=pltpu.CompilerParams(
+            collective_id=1, has_side_effects=True, vmem_limit_bytes=VMEM_LIMIT
+        ),
+        cost_estimate=pl.CostEstimate(
+            flops=4 * tokens * units * features, bytes_accessed=60_000_000, transcendentals=0
+        ),
+    )(gate_pre.reshape(blocks), up_pre.reshape(blocks), out_grad, down_weight, table)
+    gate_wide = gate_pre.astype(jnp.float32)
+    up_wide = up_pre.astype(jnp.float32)
+    sigmoid_gate = jax.nn.sigmoid(gate_wide)
+    activated = gate_wide * sigmoid_gate
+    hid_wide = hidden_grad.reshape(tokens, units).astype(jnp.float32)
+    grad_up = (hid_wide * activated).astype(wide)
+    grad_gate = (
+        hid_wide * up_wide * sigmoid_gate * (1.0 + gate_wide * (1.0 - sigmoid_gate))
+    ).astype(wide)
+    return (grad_gate, grad_up, grad_down)
+
+
+def choose(n, cores, gate_pre, up_pre, down_weight, out_grad):
+    tokens, units = gate_pre.shape
+    fits = (
+        n % 2 == 0 and n <= 16 and cores == 2
+        and tokens % (16 * n) == 0 and units % PIECE == 0 and units % 256 == 0
+        and n * units == 28 * HAD_LARGE and out_grad.shape[1] % 128 == 0
+    )
+    if fits:
+        return with_kernel(n, gate_pre, up_pre, down_weight, out_grad)
+    return per_device(gate_pre, up_pre, down_weight, out_grad)
+
+
 def solution(mesh):
     return jax.shard_map(
-        per_device,
+        functools.partial(choose, mesh.shape["tensor"], mesh.shape["dp"]),
         mesh=mesh,
         in_specs=(
             P(("groups", "dp"), "tensor"),

time: 743 us -> 374 us (0.50); the launches traced: 734 us -> 374 us
  Pallas kernels: 0 us -> 358 us
  blocking collectives: 340 us -> 0 us
  waiting for transfers between devices: 152 us -> 0 us
  matrix products: 105 us -> 0 us
  local copies, waits for them, and re-layouts: 67.3 us -> 7.44 us
  other arithmetic: 55.2 us -> 8.01 us
  between operations: 14.6 us -> 0.66 us
    pallas_call x0 -> x1, Pallas kernels: none -> 358 us  [with_kernel(): pl.pallas_call(functools.partial(whole_kernel, n), out_shape=[jax.ShapeDt...]
    all_to_all x4 -> x0, blocking collectives: 340 us -> none  [the longest x1 85.1 us: per_device(): lax.all_to_all(quant_rows, 'tensor', split_axis=1, concat_axis=0, tiled=T...]
    dot_general x6 -> x0, matrix products: 105 us -> none  [the longest x2 33 us: rotate(): jnp.einsum('ac,tad->tcd', small_table, first_section, precision=lax.Preci...]
    all_gather x1 -> x0, waiting for transfers between devices: 77.3 us -> none  [per_device(): full_grad = lax.all_gather(out_grad, 'tensor', axis=1, tiled=True)]
    reduce_scatter x1 -> x0, waiting for transfers between devices: 73.7 us -> none  [per_device(): lax.psum_scatter(partial_grad, 'dp', scatter_dimension=1, tiled=True)]
    convert_element_type x3 -> x1, other arithmetic: 49.8 us -> 8.01 us  [with_kernel(): grad_up = (hid_wide * activated).astype(wide)]
    dot_general x2 -> x0, local copies, waits for them, and re-layouts: 16 us -> none  [rotate(): jnp.dot(rows_in.reshape(row_count * small_order, large_order), large_tabl...]
    div x2 -> x0, local copies, waits for them, and re-layouts: 12.5 us -> none  [quantize(): scaled = grouped / spacing]
  transfers between devices with their start and end apart: 2 -> 0, of which waited for: 2 -> 0; matrix products, arithmetic and copies ran while one was open for 0% -> 0% of each run, Pallas kernels for 0% -> 0%
where the time goes in v2:
time: 374 us
  Pallas kernels  358 us (96%)
  other arithmetic  8.01 us (2%)
  local copies, waits for them, and re-layouts  7.44 us (2%)
    pallas_call x1, Pallas kernels, with_kernel(): pl.pallas_call(functools.partial(whole_kernel, n), out_shape=[jax.ShapeDt...  358 us
    convert_element_type x1, other arithmetic, with_kernel(): grad_up = (hid_wide * activated).astype(wide)  8.01 us

profile of v2, /device:TPU:16, one launch (start us, length us, event | category | flops | bytes accessed | tf_op | source)
XLA Modules:
  0.0 373.8 jit_solution(10919134939960304729)
XLA Ops:
  0.6 0.0 copy-start.1
  0.6 357.7 %shard_map.76 = (bf16[8,64,3584]{2,1,0:T(8,128)(2,1)}, bf16[3584,2048]{1,0:T(8,128)(2,1)}) custom-call(bf16[8,64,3584]{2,1,0:T(8,128)(2,1)} %bitcast.6, bf16[8,64,3584]{2,1,0:T(8,128)(2,1)} %bitcast.7, bf16[512,512]{1,0:T(8,128)(2,1)} %out_grad.1, bf16[3584,4096]{1,0:T(8,128)(2,1)} %weight.1, bf16[512,512]{1,0:T(8,128)(2,1)} %constant.4.clone.table), custom_call_target="tpu_custom_call" | custom-call | flops 30064771072 | bytes 60000000 | tf_op jit(solution)/shard_map/pallas_call | solution.py:396
  358.3 0.0 copy-done.1
  358.4 0.0 copy-start
  358.4 8.0 %fusion.3 = (bf16[512,3584]{1,0:T(8,128)(2,1)}, bf16[512,3584]{1,0:T(8,128)(2,1)}) fusion(bf16[512,3584]{1,0:T(8,128)(2,1)S(1)} %copy-done.1, bf16[8,64,3584]{2,1,0:T(8,128)(2,1)} %get-tuple-element.5, bf16[512,3584]{1,0:T(8,128)(2,1)} %param.6), kind=kLoop, calls=%fused_computation.8 | loop fusion | flops 29360128 | bytes 18350080 | tf_op jit(solution)/shard_map/convert_element_type | solution.py:429
  366.4 2.0 copy-done
  368.3 5.5 %copy.9 = bf16[3584,2048]{1,0:T(8,128)(2,1)} copy(bf16[3584,2048]{1,0:T(8,128)(2,1)S(1)} %copy-done) | data formatting | bytes 29360128
Async XLA Ops:
  0.6 357.7 %copy-start.1 = (bf16[512,3584]{1,0:T(8,128)(2,1)S(1)}, bf16[512,3584]{1,0:T(8,128)(2,1)}, u32[]{:S(2)}) copy-start(bf16[512,3584]{1,0:T(8,128)(2,1)} %param.5) | copy-start | bytes 11010052
  358.4 10.0 %copy-start = (bf16[3584,2048]{1,0:T(8,128)(2,1)S(1)}, bf16[3584,2048]{1,0:T(8,128)(2,1)}, u32[]{:S(2)}) copy-start(bf16[3584,2048]{1,0:T(8,128)(2,1)} %get-tuple-element.14) | copy-start | bytes 44040196

commit v3 on v2

--- a/solution.py
+++ b/solution.py
@@ -12,6 +12,7 @@
 HAD_LARGE = 1024
 GROUP = 128
 PIECE = 512
+CHUNK = 16
 MESH = pl.DeviceIdType.MESH
 ANY = pl.BlockSpec(memory_space=pl.ANY)
 VMEM_LIMIT = 60 * 1024 * 1024
@@ -130,33 +131,54 @@
     return jnp.minimum(scaled - wave * rest, 7.0) * spacing
 
 
-def exchange(n, source, target, send, recv):
+def exchange_copies(n, chunk, source, target, send, recv):
     me = lax.axis_index("tensor")
+    rows = pl.ds(pl.multiple_of(chunk * CHUNK, CHUNK), CHUNK)
     copies = []
     for step in sorted(range(1, n), key=lambda s: abs(s - n // 2)):
         peer = lax.rem(me + step, n)
-        copy = pltpu.make_async_remote_copy(
-            src_ref=source.at[peer],
-            dst_ref=target.at[me],
-            send_sem=send.at[step],
-            recv_sem=recv.at[step],
-            device_id={"tensor": peer},
-            device_id_type=MESH,
-        )
+        copies.append(
+            pltpu.make_async_remote_copy(
+                src_ref=source.at[peer, rows],
+                dst_ref=target.at[me, rows],
+                send_sem=send.at[chunk, step],
+                recv_sem=recv.at[chunk, step],
+                device_id={"tensor": peer},
+                device_id_type=MESH,
+            )
+        )
+    local = pltpu.make_async_copy(
+        source.at[me, rows], target.at[me, rows], recv.at[chunk, 0]
+    )
+    return copies, local
+
+
+def exchange(n, chunk, *refs):
+    copies, local = exchange_copies(n, chunk, *refs)
+    for copy in copies:
         copy.start()
-        copies.append(copy)
-    local = pltpu.make_async_copy(source.at[me], target.at[me], recv.at[0])
     local.start()
-    return copies, local
-
-
-def arrived(pending):
-    for copy in pending[0]:
+
+
+def arrived(n, chunk, *refs):
+    copies, local = exchange_copies(n, chunk, *refs)
+    for copy in copies:
         copy.wait_recv()
-    pending[1].wait()
-
-
-def gather_columns(n, out_grad, grad_v, sems, between):
+    local.wait()
+
+
+def sent(n, chunk, *refs):
+    for copy in exchange_copies(n, chunk, *refs)[0]:
+        copy.wait_send()
+
+
+def each_chunk(action, n, *refs):
+    @pl.loop(0, refs[0].shape[1] // CHUNK)
+    def _(chunk):
+        action(n, chunk, *refs)
+
+
+def gather_columns(n, out_grad, grad_v, sems, meanwhile, between):
     me = lax.axis_index("tensor")
     line = n // 2
     width = out_grad.shape[1]
@@ -190,6 +212,7 @@
     for sign in (1, -1):
         pl.when(has(-sign, 1))(lambda sign=sign: along(sign, 1).start())
     across(1, 0).start()
+    meanwhile()
     for hop in range(1, line):
         for sign in (1, -1):
 
@@ -200,8 +223,8 @@
                     pl.when(has(-sign, 1))(lambda: along(sign, hop + 1).start())
                 across(sign, hop).start()
 
-        if hop == 1:
-            pending = between()
+        if hop == line // 2:
+            between()
     across(1, 0).wait()
     for hop in range(1, line):
         for sign in (1, -1):
@@ -214,35 +237,34 @@
             def _(sign=sign, hop=hop):
                 along(sign, hop).wait_send()
 
-    return pending
-
-
-def rotate_pieces(n, quantized, in_v, table_v, mid_v, out_v):
-    tokens = in_v.shape[1]
+
+def rotate_pieces(n, quantized, chunk, in_v, table_v, mid_v, out_v):
+    tokens = CHUNK
     per = in_v.shape[2] // PIECE
     scale = 1.0 / math.sqrt(n * per * PIECE)
-
-    @pl.loop(0, n)
-    def _(at):
-        block = in_v[at]
-        stacked = jnp.concatenate(
-            [block[:, PIECE * k : PIECE * (k + 1)] for k in range(per)], axis=0
-        )
-        first = jnp.dot(stacked, table_v[...], preferred_element_type=jnp.float32)
-        mid_v[pl.ds(at * per, per)] = first.reshape(per, tokens, PIECE)
+    rows = pl.ds(pl.multiple_of(chunk * CHUNK, CHUNK), CHUNK)
+    stacked = jnp.concatenate(
+        [
+            in_v[at, rows, PIECE * k : PIECE * (k + 1)]
+            for at in range(n)
+            for k in range(per)
+        ],
+        axis=0,
+    )
+    first = jnp.dot(stacked, table_v[...], preferred_element_type=jnp.float32)
+    mid_v[...] = first.reshape(n * per, tokens, PIECE)
 
     signs = conference()
     order = signs.shape[0]
     lane_tiles = PIECE // GROUP
 
-    @pl.loop(0, tokens // 16 * lane_tiles)
+    @pl.loop(0, lane_tiles)
     def _(step):
-        rows = pl.ds(pl.multiple_of((step // lane_tiles) * 16, 16), 16)
-        lane = (step % lane_tiles) * GROUP
+        lane = step * GROUP
         lanes = pl.ds(pl.multiple_of(lane, GROUP), GROUP)
 
         def total(i, j, half):
-            even, odd = mid_v[i * 4 + j * 2, rows, lanes], mid_v[i * 4 + j * 2 + 1, rows, lanes]
+            even, odd = mid_v[i * 4 + j * 2, :, lanes], mid_v[i * 4 + j * 2 + 1, :, lanes]
             return even - odd if half else even + odd
 
         for half in range(2):
@@ -299,6 +321,18 @@
     greet(n, sibling=True)
     loads[3].wait()
 
+    to_tokens, grads_to_tokens, levels, grads_back = [
+        (source, target, send.at[at], recv.at[at])
+        for at, (source, target) in enumerate(
+            [
+                (hidden_v, token_v),
+                (rot_v, back_in_v),
+                (out_v, quant_v.at[pl.ds(0, n)]),
+                (back_v, hidden_grad),
+            ]
+        )
+    ]
+
     def make_hidden():
         loads[0].wait()
         loads[1].wait()
@@ -313,9 +347,10 @@
                 hidden_v.dtype
             )
 
-        return exchange(n, hidden_v, token_v, send.at[0], recv.at[0])
-
-    to_tokens = gather_columns(n, out_grad, grad_v, gather_sem, make_hidden)
+    def send_hidden():
+        each_chunk(exchange, n, *to_tokens)
+
+    gather_columns(n, out_grad, grad_v, gather_sem, make_hidden, send_hidden)
 
     @pl.loop(0, tiles)
     def _(tile):
@@ -328,7 +363,7 @@
         )
         rot_v[:, :, units] = product.astype(rot_v.dtype).reshape(n, part, 256)
 
-    grads_to_tokens = exchange(n, rot_v, back_in_v, send.at[1], recv.at[1])
+    each_chunk(exchange, n, *grads_to_tokens)
 
     def beside(which):
         return grad_v.at[:, pl.ds(pl.multiple_of(which * half, half), half)]
@@ -347,15 +382,21 @@
 
     side_grad = to_sibling(beside(1 - core), side_grad_v, 0)
     loads[2].wait()
-    arrived(to_tokens)
-    rotate_pieces(n, True, token_v, table_v, mid_v, out_v)
-    own_levels = quant_v.at[pl.ds(0, n)]
-    levels = exchange(n, out_v, own_levels, send.at[2], recv.at[2])
-    arrived(grads_to_tokens)
-    rotate_pieces(n, False, back_in_v, table_v, mid_v, back_v)
-    grads_back = exchange(n, back_v, hidden_grad, send.at[3], recv.at[3])
-    arrived(levels)
-    side_levels = to_sibling(own_levels, quant_v.at[pl.ds(n, n)], 1)
+
+    @pl.loop(0, part // CHUNK)
+    def _(chunk):
+        arrived(n, chunk, *to_tokens)
+        rotate_pieces(n, True, chunk, token_v, table_v, mid_v, out_v)
+        exchange(n, chunk, *levels)
+
+    @pl.loop(0, part // CHUNK)
+    def _(chunk):
+        arrived(n, chunk, *grads_to_tokens)
+        rotate_pieces(n, False, chunk, back_in_v, table_v, mid_v, back_v)
+        exchange(n, chunk, *grads_back)
+
+    each_chunk(arrived, n, *levels)
+    side_levels = to_sibling(quant_v.at[pl.ds(0, n)], quant_v.at[pl.ds(n, n)], 1)
     side_grad.wait()
     side_levels.wait()
 
@@ -378,10 +419,9 @@
 
     for tile in range(max(tiles - 2, 0), tiles):
         write(tile).wait()
-    arrived(grads_back)
-    for copies, _ in (to_tokens, grads_to_tokens, levels, grads_back):
-        for copy in copies:
-            copy.wait_send()
+    each_chunk(arrived, n, *grads_back)
+    for refs in (to_tokens, grads_to_tokens, levels, grads_back):
+        each_chunk(sent, n, *refs)
 
 
 def with_kernel(n, gate_pre, up_pre, down_weight, out_grad):
@@ -403,7 +443,7 @@
         out_specs=[ANY] * 2,
         scratch_shapes=[
             keep, keep, keep, keep,
-            pltpu.VMEM((n * units // PIECE, part, PIECE), jnp.float32),
+            pltpu.VMEM((n * units // PIECE, CHUNK, PIECE), jnp.float32),
             keep, keep,
             pltpu.VMEM((2 * n, part, units), wide),
             pltpu.VMEM((tokens, features), wide),
@@ -411,7 +451,7 @@
             pltpu.VMEM((2, 256, features), wide),
             pltpu.VMEM((2, 256, features // 2), wide),
             pltpu.VMEM((PIECE, PIECE), wide),
-            dma((2, 2 * n)), dma((4, n)), dma((4, n)), dma((2,)), dma((2,)),
+            dma((2, 2 * n)), dma((4, part // CHUNK, n)), dma((4, part // CHUNK, n)), dma((2,)), dma((2,)),
             dma((4,)), dma((2,)), dma((2,)),
         ],
         compiler_params=pltpu.CompilerParams(
@@ -436,8 +476,8 @@
 def choose(n, cores, gate_pre, up_pre, down_weight, out_grad):
     tokens, units = gate_pre.shape
     fits = (
-        n % 2 == 0 and n <= 16 and cores == 2
-        and tokens % (16 * n) == 0 and units % PIECE == 0 and units % 256 == 0
+        n % 2 == 0 and 4 <= n <= 16 and cores == 2
+        and tokens % (CHUNK * n) == 0 and units % PIECE == 0 and units % 256 == 0
         and n * units == 28 * HAD_LARGE and out_grad.shape[1] % 128 == 0
     )
     if fits:

time: 374 us -> 366 us (0.979)
  Pallas kernels: 358 us -> 349 us
    pallas_call x1, Pallas kernels: 358 us -> 349 us  [with_kernel(): pl.pallas_call(functools.partial(whole_kernel, n), out_shape=[jax.ShapeDt...]
where the time goes in v3:
time: 366 us; the launch traced here: 365 us
  Pallas kernels  349 us (95%)
  other arithmetic  8.01 us (2%)
  local copies, waits for them, and re-layouts  7.44 us (2%)
    pallas_call x1, Pallas kernels, with_kernel(): pl.pallas_call(functools.partial(whole_kernel, n), out_shape=[jax.ShapeDt...  349 us
    convert_element_type x1, other arithmetic, with_kernel(): grad_up = (hid_wide * activated).astype(wide)  8.01 us
    unnamed x5, local copies, waits for them, and re-layouts  7.44 us

profile of v3, /device:TPU:16, one launch (start us, length us, event | category | flops | bytes accessed | tf_op | source)
XLA Modules:
  0.0 365.1 jit_solution(18078858914780582611)
XLA Ops:
  0.6 0.0 copy-start.1
  0.6 348.9 %shard_map.76 = (bf16[8,64,3584]{2,1,0:T(8,128)(2,1)}, bf16[3584,2048]{1,0:T(8,128)(2,1)}) custom-call(bf16[8,64,3584]{2,1,0:T(8,128)(2,1)} %bitcast.6, bf16[8,64,3584]{2,1,0:T(8,128)(2,1)} %bitcast.7, bf16[512,512]{1,0:T(8,128)(2,1)} %out_grad.1, bf16[3584,4096]{1,0:T(8,128)(2,1)} %weight.1, bf16[512,512]{1,0:T(8,128)(2,1)} %constant.4.clone.table), custom_call_target="tpu_custom_call" | custom-call | flops 30064771072 | bytes 60000000 | tf_op jit(solution)/shard_map/pallas_call | solution.py:436
  349.6 0.0 copy-done.1
  349.6 0.0 copy-start
  349.6 8.0 %fusion.3 = (bf16[512,3584]{1,0:T(8,128)(2,1)}, bf16[512,3584]{1,0:T(8,128)(2,1)}) fusion(bf16[512,3584]{1,0:T(8,128)(2,1)S(1)} %copy-done.1, bf16[8,64,3584]{2,1,0:T(8,128)(2,1)} %get-tuple-element.5, bf16[512,3584]{1,0:T(8,128)(2,1)} %param.6), kind=kLoop, calls=%fused_computation.8 | loop fusion | flops 29360128 | bytes 18350080 | tf_op jit(solution)/shard_map/convert_element_type | solution.py:469
  357.6 2.0 copy-done
  359.6 5.5 %copy.9 = bf16[3584,2048]{1,0:T(8,128)(2,1)} copy(bf16[3584,2048]{1,0:T(8,128)(2,1)S(1)} %copy-done) | data formatting | bytes 29360128
Async XLA Ops:
  0.6 349.0 %copy-start.1 = (bf16[512,3584]{1,0:T(8,128)(2,1)S(1)}, bf16[512,3584]{1,0:T(8,128)(2,1)}, u32[]{:S(2)}) copy-start(bf16[512,3584]{1,0:T(8,128)(2,1)} %param.5) | copy-start | bytes 11010052
  349.6 10.0 %copy-start = (bf16[3584,2048]{1,0:T(8,128)(2,1)S(1)}, bf16[3584,2048]{1,0:T(8,128)(2,1)}, u32[]{:S(2)}) copy-start(bf16[3584,2048]{1,0:T(8,128)(2,1)} %get-tuple-element.14) | copy-start | bytes 44040196

commit v4 on v3

--- a/solution.py
+++ b/solution.py
@@ -352,6 +352,31 @@
 
     gather_columns(n, out_grad, grad_v, gather_sem, make_hidden, send_hidden)
 
+
+    def beside(which):
+        return grad_v.at[:, pl.ds(pl.multiple_of(which * half, half), half)]
+
+    def to_sibling(source, target, at):
+        copy = pltpu.make_async_remote_copy(
+            src_ref=source,
+            dst_ref=target,
+            send_sem=side_send.at[at],
+            recv_sem=side_recv.at[at],
+            device_id={"dp": 1 - core},
+            device_id_type=MESH,
+        )
+        copy.start()
+        return copy
+
+    side_grad = to_sibling(beside(1 - core), side_grad_v, 0)
+    loads[2].wait()
+
+    @pl.loop(0, part // CHUNK)
+    def _(chunk):
+        arrived(n, chunk, *to_tokens)
+        rotate_pieces(n, True, chunk, token_v, table_v, mid_v, out_v)
+        exchange(n, chunk, *levels)
+
     @pl.loop(0, tiles)
     def _(tile):
         pl.when(tile + 1 < tiles)(lambda: fetch(tile + 1).start())
@@ -364,30 +389,6 @@
         rot_v[:, :, units] = product.astype(rot_v.dtype).reshape(n, part, 256)
 
     each_chunk(exchange, n, *grads_to_tokens)
-
-    def beside(which):
-        return grad_v.at[:, pl.ds(pl.multiple_of(which * half, half), half)]
-
-    def to_sibling(source, target, at):
-        copy = pltpu.make_async_remote_copy(
-            src_ref=source,
-            dst_ref=target,
-            send_sem=side_send.at[at],
-            recv_sem=side_recv.at[at],
-            device_id={"dp": 1 - core},
-            device_id_type=MESH,
-        )
-        copy.start()
-        return copy
-
-    side_grad = to_sibling(beside(1 - core), side_grad_v, 0)
-    loads[2].wait()
-
-    @pl.loop(0, part // CHUNK)
-    def _(chunk):
-        arrived(n, chunk, *to_tokens)
-        rotate_pieces(n, True, chunk, token_v, table_v, mid_v, out_v)
-        exchange(n, chunk, *levels)
 
     @pl.loop(0, part // CHUNK)
     def _(chunk):

time: 366 us -> 367 us (level)
  no operation moved by 1% of the time
where the time goes in v4:
time: 367 us; the launch traced here: 366 us
  Pallas kernels  350 us (95%)
  other arithmetic  8.01 us (2%)
  local copies, waits for them, and re-layouts  7.44 us (2%)
    pallas_call x1, Pallas kernels, with_kernel(): pl.pallas_call(functools.partial(whole_kernel, n), out_shape=[jax.ShapeDt...  350 us
    convert_element_type x1, other arithmetic, with_kernel(): grad_up = (hid_wide * activated).astype(wide)  8.01 us
    unnamed x5, local copies, waits for them, and re-layouts  7.44 us

profile of v4, /device:TPU:16, one launch (start us, length us, event | category | flops | bytes accessed | tf_op | source)
XLA Modules:
  0.0 366.3 jit_solution(5084388847122352460)
XLA Ops:
  0.6 0.0 copy-start.1
  0.6 350.2 %shard_map.76 = (bf16[8,64,3584]{2,1,0:T(8,128)(2,1)}, bf16[3584,2048]{1,0:T(8,128)(2,1)}) custom-call(bf16[8,64,3584]{2,1,0:T(8,128)(2,1)} %bitcast.6, bf16[8,64,3584]{2,1,0:T(8,128)(2,1)} %bitcast.7, bf16[512,512]{1,0:T(8,128)(2,1)} %out_grad.1, bf16[3584,4096]{1,0:T(8,128)(2,1)} %weight.1, bf16[512,512]{1,0:T(8,128)(2,1)} %constant.4.clone.table), custom_call_target="tpu_custom_call" | custom-call | flops 30064771072 | bytes 60000000 | tf_op jit(solution)/shard_map/pallas_call | solution.py:437
  350.8 0.0 copy-done.1
  350.8 0.0 copy-start
  350.8 8.0 %fusion.3 = (bf16[512,3584]{1,0:T(8,128)(2,1)}, bf16[512,3584]{1,0:T(8,128)(2,1)}) fusion(bf16[512,3584]{1,0:T(8,128)(2,1)S(1)} %copy-done.1, bf16[8,64,3584]{2,1,0:T(8,128)(2,1)} %get-tuple-element.5, bf16[512,3584]{1,0:T(8,128)(2,1)} %param.6), kind=kLoop, calls=%fused_computation.8 | loop fusion | flops 29360128 | bytes 18350080 | tf_op jit(solution)/shard_map/convert_element_type | solution.py:470
  358.9 2.0 copy-done
  360.8 5.5 %copy.9 = bf16[3584,2048]{1,0:T(8,128)(2,1)} copy(bf16[3584,2048]{1,0:T(8,128)(2,1)S(1)} %copy-done) | data formatting | bytes 29360128
Async XLA Ops:
  0.6 350.2 %copy-start.1 = (bf16[512,3584]{1,0:T(8,128)(2,1)S(1)}, bf16[512,3584]{1,0:T(8,128)(2,1)}, u32[]{:S(2)}) copy-start(bf16[512,3584]{1,0:T(8,128)(2,1)} %param.5) | copy-start | bytes 11010052
  350.8 10.0 %copy-start = (bf16[3584,2048]{1,0:T(8,128)(2,1)S(1)}, bf16[3584,2048]{1,0:T(8,128)(2,1)}, u32[]{:S(2)}) copy-start(bf16[3584,2048]{1,0:T(8,128)(2,1)} %get-tuple-element.14) | copy-start | bytes 44040196
